TPU v7x, 32 devices: a whole 2x2x4 slice. The times are simulated.
32 devices in a mesh: groups: 2 (over y), doc: 16 (over z, x, core).
Axes of the slice: x: 2, y: 2, z: 4, core: 2. Of those that a mesh axis runs over, the one named last changes fastest.
Arguments:
- queries: bfloat16 [32, 32, 128], P(('groups', 'doc')), parts along dimension 0, may hold values from -0.015625 to 0.015625
- doc_tokens: bfloat16 [4096, 128, 128], P(('groups', 'doc')), parts along dimension 0, may hold values from -6 to 6
- doc_lengths: int32 [4096], P(('groups', 'doc')), parts along dimension 0, may hold values from 1 to 128, as said below
- candidates: int32 [32, 256], P(('groups', 'doc')), parts along dimension 0, may hold values from 0 to 2047, as said below
Outputs:
- scores: float32 [32, 256], P(('groups', 'doc')), parts along dimension 0
There are 2 independent parts, one for each index of `groups`. A program takes and returns all parts, laid end to end along the dimension named above; each array names one. Nothing has to cross between parts.
Inputs may be any that keep to these rules, and one draw needn't show every extreme that they name: Passage ids. Device d holds passages d * 128 to (d + 1) * 128 - 1 and queries d * 1 to (d + 1) - 1. At most 48 candidates of one query lie on any one device; in every draw one device holds exactly 48 candidates of every query. A query may name a passage more than once. `doc_lengths`: the first passage of every device has all 128 tokens.
All inputs are finite; a program needn't handle non-finite values.
Results may differ from a plain program's by a relative error of at most 0.0003.
Values may be sent and summed in bfloat16 or wider, within the bound.
A program may use at most 64 MiB of HBM per device.

v0:
```python
import jax
import jax.numpy as jnp
from jax import lax
from jax.sharding import PartitionSpec as P


def block_rows(total, limit):
    width = max(1, min(total, limit))
    while total % width != 0:
        width = width - 1
    return width


def body(queries, doc_tokens, doc_lengths, candidates):
    devices = lax.axis_size("doc")
    local_queries, query_len, feature = queries.shape
    cand_count = candidates.shape[1]
    local_docs = doc_tokens.shape[0]
    doc_len = doc_tokens.shape[1]
    most = max(2, (3 * cand_count + devices - 1) // devices)
    query_rows = queries.reshape(local_queries, query_len * feature)
    owners = candidates // local_docs
    hits = (owners[:, :, None] == jnp.arange(devices, dtype=jnp.int32)[None, None, :]).astype(
        jnp.int32
    )
    before = jnp.sum((jnp.cumsum(hits, axis=1) - hits) * hits, axis=2)
    query_ids = jnp.arange(local_queries, dtype=jnp.int32)[:, None]
    slot_of = (owners * local_queries + query_ids) * most + before
    table = (
        jnp.full((devices * local_queries * most,), -1, jnp.int32)
        .at[slot_of.reshape(-1)]
        .set((candidates % local_docs).reshape(-1))
    )
    send_docs = table.reshape(devices, local_queries, most)
    send_rows = jnp.broadcast_to(
        query_rows[None, :, :], (devices, local_queries, query_len * feature)
    )
    got_rows = lax.all_to_all(send_rows, "doc", split_axis=0, concat_axis=0, tiled=True)
    got_docs = lax.all_to_all(send_docs, "doc", split_axis=0, concat_axis=0, tiled=True)
    width = got_rows.shape[1]
    row_block = got_rows.reshape(devices * width, got_rows.shape[2])
    doc_table = got_docs.reshape(devices * width, most)
    total_rows = row_block.shape[0]
    slots = doc_table.shape[1]
    maxsim_width = block_rows(total_rows, max(1, 256 // slots))

    def score_block(packed):
        block_queries, block_docs = packed
        safe_docs = jnp.maximum(block_docs, 0)
        doc_block = doc_tokens[safe_docs]
        block_lengths = doc_lengths[safe_docs]
        similar = jnp.einsum(
            "bak,bctk->bcat",
            block_queries.reshape(maxsim_width, query_len, feature),
            doc_block,
            preferred_element_type=jnp.float32,
        )
        keep = jnp.arange(doc_len)[None, None, None, :] < block_lengths[:, :, None, None]
        best = jnp.max(jnp.where(keep, similar, -jnp.inf), axis=3)
        return jnp.where(block_docs >= 0, jnp.sum(best, axis=2), 0.0)

    scored = lax.map(
        score_block,
        (
            row_block.reshape(total_rows // maxsim_width, maxsim_width, row_block.shape[1]),
            doc_table.reshape(total_rows // maxsim_width, maxsim_width, slots),
        ),
    )
    got_scores = scored.reshape(total_rows, slots).reshape(devices, width, most)
    returned = lax.all_to_all(got_scores, "doc", split_axis=0, concat_axis=0, tiled=True)
    result = returned.reshape(devices * local_queries * most)[slot_of.reshape(-1)].reshape(
        local_queries, cand_count
    )
    return result


def solution(mesh):
    placed = (
        P(("groups", "doc"), None, None),
        P(("groups", "doc"), None, None),
        P(("groups", "doc")),
        P(("groups", "doc"), None),
    )
    return jax.shard_map(
        body, mesh=mesh, in_specs=placed, out_specs=P(("groups", "doc"), None), check_vma=False
    )
```

profile of v0, /device:TPU:0, one launch (start us, length us, event | category | flops | bytes accessed | tf_op | source)
XLA Modules:
  0.0 113.2 jit_solution(13427673627998278382)
XLA Ops:
  0.0 0.9 broadcast_in_dim.42
  0.9 0.5 broadcast.152
  1.4 1.4 %reduce.9 = bf16[16,4096]{1,0:T(8,128)(2,1)S(1)} reduce(bf16[16,1,4096]{2,1,0:T(2,128)(2,1)S(1)} %broadcast_in_dim.42, bf16[]{:T(256)} %broadcast.152), dimensions={1}, to_apply=%broadcast_in_dim.42.reduce_sub_computation | reduce | bytes 262146 | tf_op jit(solution)/shard_map/broadcast_in_dim | solution.py:35
  2.8 0.7 reshape.240
  3.5 7.4 %all-to-all-start.1 = ((bf16[16,2,2048]{2,1,0:T(2,128)(2,1)}), bf16[16,2,2048]{2,1,0:T(2,128)(2,1)S(1)}, u32[]{:S(2)}, u32[]{:S(2)}) async-start(bf16[16,2,2048]{2,1,0:T(2,128)(2,1)} %reshape.240), calls=%async_computation.1 | async-start | bytes 262144 | tf_op jit(solution)/shard_map/all_to_all | solution.py:38
  10.9 0.7 and_select_fusion
  11.6 0.7 and_select_fusion.1
  12.3 0.6 reduce-window.6
  12.9 0.2 slice_reduce_fusion
  13.1 0.1 copy.20
  13.3 1.4 %scatter_custom_fusion = s32[768]{0:T(1024)S(1)} fusion(s32[256]{0:T(256)S(1)} %bitcast.61, s32[256]{0:T(256)S(1)} %bitcast.65, s32[]{:T(128)} %constant.52.clone.1), kind=kCustom, calls=%fused_computation.25 | custom fusion | bytes 3076 | tf_op jit(solution)/shard_map/scatter | solution.py:32
  14.8 0.7 reshape.186
  15.4 3.4 %all-to-all-done.1 = bf16[16,2,2048]{2,1,0:T(2,128)(2,1)S(1)} async-done(((bf16[16,2,2048]{2,1,0:T(2,128)(2,1)}), bf16[16,2,2048]{2,1,0:T(2,128)(2,1)S(1)}, u32[]{:S(2)}, u32[]{:S(2)}) %all-to-all-start.1) | async-done | bytes 131104 | tf_op jit(solution)/shard_map/all_to_all | solution.py:38
  18.8 3.4 %all-to-all-start = ((s32[16,1,48]{2,1,0:T(1,128)}), s32[16,1,48]{2,1,0:T(1,128)S(1)}, u32[]{:S(2)}, u32[]{:S(2)}) async-start(s32[16,1,48]{2,1,0:T(1,128)} %reshape.186), calls=%async_computation | async-start | bytes 16384 | tf_op jit(solution)/shard_map/all_to_all | solution.py:39
  22.2 0.1 reshape.241
  22.4 0.7 reduce.3
  23.2 5.4 %all-to-all-done = s32[16,1,48]{2,1,0:T(1,128)S(1)} async-done(((s32[16,1,48]{2,1,0:T(1,128)}), s32[16,1,48]{2,1,0:T(1,128)S(1)}, u32[]{:S(2)}, u32[]{:S(2)}) %all-to-all-start) | async-done | bytes 3104 | tf_op jit(solution)/shard_map/all_to_all | solution.py:39
  28.6 71.6 %while.10 = (s32[]{:T(128)}, f32[4,4,48]{2,1,0:T(4,128)}, s32[4,4,48]{2,1,0:T(4,128)S(1)}, s32[128]{0:T(128)}, bf16[128,128,128]{2,1,0:T(8,128)(2,1)}, /*index=5...) while((s32[]{:T(128)}, f32[4,4,48]{2,1,0:T(4,128)}, s32[4,4,48]{2,1,0:T(4,128)S(1)}, s32[128]{0:T(128)}, ...), condition=%wide.region_7.8_spmd, body=%wide.region_4.7_spmd.sunk | while | flops 202925440 | bytes 19091324 | solution.py:62
  28.6 0.1 reshape.252
  28.7 10.2 %gather_fusion = bf16[192,128,128]{2,1,0:T(8,128)(2,1)} fusion(bf16[128,128,128]{2,1,0:T(8,128)(2,1)} %get-tuple-element.109, s32[1024]{0:T(1024)S(1)} %pad_clamp_fusion.3), kind=kCustom, calls=%fused_computation.1.clone.1 | custom fusion | bytes 12583680 | tf_op jit(solution)/shard_map/while/body/eval_jaxpr/gather | solution.py:50
  38.9 1.5 %gather_fusion.1 = s32[192]{0:T(256)S(1)} fusion(s32[128]{0:T(128)S(1)} %copy-done, s32[1024]{0:T(1024)S(1)} %pad_clamp_fusion.3), kind=kCustom, calls=%fused_computation.clone.1 | custom fusion | bytes 2304 | tf_op jit(solution)/shard_map/while/body/eval_jaxpr/gather | solution.py:51
  40.5 0.1 iota_compare_fusion.2
  40.6 5.1 %select_reduce_fusion.2 = f32[4,48,32]{2,1,0:T(8,128)S(1)} fusion(bf16[4,48,128,128]{3,2,1,0:T(8,128)(2,1)} %bitcast.53, pred[4,48,128]{2,1,0:T(8,128)(4,1)S(1)} %iota_compare_fusion.2, bf16[1,4,32,128]{3,1,2,0:T(4,128)(2,1)S(1)} %dynamic-slice_bitcast_fusion.2), kind=kOutput, calls=%fused_computation.4.clone.1 | convolution fusion | flops 202893312 | bytes 6373376 | tf_op jit(solution)/shard_map/while/body/eval_jaxpr/bak,bctk->bcat/dot_general | solution.py:52
  45.8 0.1 reduce_sum.26
  45.9 0.6 fusion.9
  46.6 10.2 %gather_fusion = bf16[192,128,128]{2,1,0:T(8,128)(2,1)} fusion(bf16[128,128,128]{2,1,0:T(8,128)(2,1)} %get-tuple-element.109, s32[1024]{0:T(1024)S(1)} %pad_clamp_fusion.3), kind=kCustom, calls=%fused_computation.1.clone.1 | custom fusion | bytes 12583680 | tf_op jit(solution)/shard_map/while/body/eval_jaxpr/gather | solution.py:50
  56.8 1.5 %gather_fusion.1 = s32[192]{0:T(256)S(1)} fusion(s32[128]{0:T(128)S(1)} %copy-done, s32[1024]{0:T(1024)S(1)} %pad_clamp_fusion.3), kind=kCustom, calls=%fused_computation.clone.1 | custom fusion | bytes 2304 | tf_op jit(solution)/shard_map/while/body/eval_jaxpr/gather | solution.py:51
  58.4 0.1 iota_compare_fusion.2
  58.5 5.1 %select_reduce_fusion.2 = f32[4,48,32]{2,1,0:T(8,128)S(1)} fusion(bf16[4,48,128,128]{3,2,1,0:T(8,128)(2,1)} %bitcast.53, pred[4,48,128]{2,1,0:T(8,128)(4,1)S(1)} %iota_compare_fusion.2, bf16[1,4,32,128]{3,1,2,0:T(4,128)(2,1)S(1)} %dynamic-slice_bitcast_fusion.2), kind=kOutput, calls=%fused_computation.4.clone.1 | convolution fusion | flops 202893312 | bytes 6373376 | tf_op jit(solution)/shard_map/while/body/eval_jaxpr/bak,bctk->bcat/dot_general | solution.py:52
  63.7 0.1 reduce_sum.26
  63.8 0.6 fusion.9
  64.5 10.2 %gather_fusion = bf16[192,128,128]{2,1,0:T(8,128)(2,1)} fusion(bf16[128,128,128]{2,1,0:T(8,128)(2,1)} %get-tuple-element.109, s32[1024]{0:T(1024)S(1)} %pad_clamp_fusion.3), kind=kCustom, calls=%fused_computation.1.clone.1 | custom fusion | bytes 12583680 | tf_op jit(solution)/shard_map/while/body/eval_jaxpr/gather | solution.py:50
  74.6 1.5 %gather_fusion.1 = s32[192]{0:T(256)S(1)} fusion(s32[128]{0:T(128)S(1)} %copy-done, s32[1024]{0:T(1024)S(1)} %pad_clamp_fusion.3), kind=kCustom, calls=%fused_computation.clone.1 | custom fusion | bytes 2304 | tf_op jit(solution)/shard_map/while/body/eval_jaxpr/gather | solution.py:51
  76.3 0.1 iota_compare_fusion.2
  76.4 5.1 %select_reduce_fusion.2 = f32[4,48,32]{2,1,0:T(8,128)S(1)} fusion(bf16[4,48,128,128]{3,2,1,0:T(8,128)(2,1)} %bitcast.53, pred[4,48,128]{2,1,0:T(8,128)(4,1)S(1)} %iota_compare_fusion.2, bf16[1,4,32,128]{3,1,2,0:T(4,128)(2,1)S(1)} %dynamic-slice_bitcast_fusion.2), kind=kOutput, calls=%fused_computation.4.clone.1 | convolution fusion | flops 202893312 | bytes 6373376 | tf_op jit(solution)/shard_map/while/body/eval_jaxpr/bak,bctk->bcat/dot_general | solution.py:52
  81.6 0.1 reduce_sum.26
  81.7 0.6 fusion.9
  82.4 10.2 %gather_fusion = bf16[192,128,128]{2,1,0:T(8,128)(2,1)} fusion(bf16[128,128,128]{2,1,0:T(8,128)(2,1)} %get-tuple-element.109, s32[1024]{0:T(1024)S(1)} %pad_clamp_fusion.3), kind=kCustom, calls=%fused_computation.1.clone.1 | custom fusion | bytes 12583680 | tf_op jit(solution)/shard_map/while/body/eval_jaxpr/gather | solution.py:50
  92.6 1.5 %gather_fusion.1 = s32[192]{0:T(256)S(1)} fusion(s32[128]{0:T(128)S(1)} %copy-done, s32[1024]{0:T(1024)S(1)} %pad_clamp_fusion.3), kind=kCustom, calls=%fused_computation.clone.1 | custom fusion | bytes 2304 | tf_op jit(solution)/shard_map/while/body/eval_jaxpr/gather | solution.py:51
  94.2 0.1 iota_compare_fusion.2
  94.3 5.1 %select_reduce_fusion.2 = f32[4,48,32]{2,1,0:T(8,128)S(1)} fusion(bf16[4,48,128,128]{3,2,1,0:T(8,128)(2,1)} %bitcast.53, pred[4,48,128]{2,1,0:T(8,128)(4,1)S(1)} %iota_compare_fusion.2, bf16[1,4,32,128]{3,1,2,0:T(4,128)(2,1)S(1)} %dynamic-slice_bitcast_fusion.2), kind=kOutput, calls=%fused_computation.4.clone.1 | convolution fusion | flops 202893312 | bytes 6373376 | tf_op jit(solution)/shard_map/while/body/eval_jaxpr/bak,bctk->bcat/dot_general | solution.py:52
  99.5 0.1 reduce_sum.26
  99.6 0.6 fusion.9
  100.2 3.4 %all-to-all-start.2 = ((f32[16,1,48]{2,1,0:T(1,128)}), f32[16,1,48]{2,1,0:T(1,128)S(1)}, u32[]{:S(2)}, u32[]{:S(2)}) async-start(f32[16,1,48]{2,1,0:T(1,128)} %bitcast.16), calls=%async_computation.2 | async-start | bytes 16384 | tf_op jit(solution)/shard_map/all_to_all | solution.py:70
  103.6 6.4 %all-to-all-done.2 = f32[16,1,48]{2,1,0:T(1,128)S(1)} async-done(((f32[16,1,48]{2,1,0:T(1,128)}), f32[16,1,48]{2,1,0:T(1,128)S(1)}, u32[]{:S(2)}, u32[]{:S(2)}) %all-to-all-start.2) | async-done | bytes 3104 | tf_op jit(solution)/shard_map/all_to_all | solution.py:70
  110.0 0.5 broadcast.150
  110.5 0.7 reduce.8
  111.2 1.9 %gather_fusion.2 = f32[256]{0:T(256)} fusion(f32[768]{0:T(1024)S(1)} %reshape.187, s32[1024]{0:T(1024)S(1)} %pad_clamp_fusion.1), kind=kCustom, calls=%fused_computation.2 | custom fusion | bytes 3072 | tf_op jit(solution)/shard_map/gather | solution.py:71
  (39 shorter events, 1.1 us)
Async XLA Ops:
  3.5 15.3 %all-to-all-start.1 = ((bf16[16,2,2048]{2,1,0:T(2,128)(2,1)}), bf16[16,2,2048]{2,1,0:T(2,128)(2,1)S(1)}, u32[]{:S(2)}, u32[]{:S(2)}) async-start(bf16[16,2,2048]{2,1,0:T(2,128)(2,1)} %reshape.240), calls=%async_computation.1 | async-start | bytes 262144 | tf_op jit(solution)/shard_map/all_to_all | solution.py:38
  18.8 9.8 %all-to-all-start = ((s32[16,1,48]{2,1,0:T(1,128)}), s32[16,1,48]{2,1,0:T(1,128)S(1)}, u32[]{:S(2)}, u32[]{:S(2)}) async-start(s32[16,1,48]{2,1,0:T(1,128)} %reshape.186), calls=%async_computation | async-start | bytes 16384 | tf_op jit(solution)/shard_map/all_to_all | solution.py:39
  28.7 10.2 %copy-start = (s32[128]{0:T(128)S(1)}, s32[128]{0:T(128)}, u32[]{:S(2)}) copy-start(s32[128]{0:T(128)} %get-tuple-element.108) | copy-start | bytes 1540 | tf_op jit(solution)/shard_map/while
  46.6 10.2 %copy-start = (s32[128]{0:T(128)S(1)}, s32[128]{0:T(128)}, u32[]{:S(2)}) copy-start(s32[128]{0:T(128)} %get-tuple-element.108) | copy-start | bytes 1540 | tf_op jit(solution)/shard_map/while
  64.5 10.2 %copy-start = (s32[128]{0:T(128)S(1)}, s32[128]{0:T(128)}, u32[]{:S(2)}) copy-start(s32[128]{0:T(128)} %get-tuple-element.108) | copy-start | bytes 1540 | tf_op jit(solution)/shard_map/while
  82.3 10.2 %copy-start = (s32[128]{0:T(128)S(1)}, s32[128]{0:T(128)}, u32[]{:S(2)}) copy-start(s32[128]{0:T(128)} %get-tuple-element.108) | copy-start | bytes 1540 | tf_op jit(solution)/shard_map/while
  100.2 9.8 %all-to-all-start.2 = ((f32[16,1,48]{2,1,0:T(1,128)}), f32[16,1,48]{2,1,0:T(1,128)S(1)}, u32[]{:S(2)}, u32[]{:S(2)}) async-start(f32[16,1,48]{2,1,0:T(1,128)} %bitcast.16), calls=%async_computation.2 | async-start | bytes 16384 | tf_op jit(solution)/shard_map/all_to_all | solution.py:70
where the time goes:
time: 114 us; the launch traced here: 113 us
  local copies, waits for them, and re-layouts  54.9 us (48%)
  matrix products  20.5 us (18%)
  waiting for transfers between devices  15.1 us (13%)
  starting transfers between devices  14.2 us (12%)
  other arithmetic  8.09 us (7%)
    gather x4, local copies, waits for them, and re-layouts, score_block(): doc_block = doc_tokens[safe_docs]  40.7 us
    dot_general x4, matrix products, score_block(): jnp.einsum('bak,bctk->bcat', block_queries.reshape(maxsim_width, query_le...  20.5 us
    all_to_all x1, starting transfers between devices, body(): lax.all_to_all(send_rows, 'doc', split_axis=0, concat_axis=0, tiled=True)  7.36 us
    gather x8, local copies, waits for them, and re-layouts, score_block(): block_lengths = doc_lengths[safe_docs]  6.53 us
    all_to_all x1, waiting for transfers between devices, body(): lax.all_to_all(got_scores, 'doc', split_axis=0, concat_axis=0, tiled=True)  6.36 us
    all_to_all x1, waiting for transfers between devices, body(): lax.all_to_all(send_docs, 'doc', split_axis=0, concat_axis=0, tiled=True)  5.42 us
    all_to_all x1, starting transfers between devices, body(): lax.all_to_all(got_scores, 'doc', split_axis=0, concat_axis=0, tiled=True)  3.42 us
    all_to_all x1, starting transfers between devices, body(): lax.all_to_all(send_docs, 'doc', split_axis=0, concat_axis=0, tiled=True)  3.41 us
  transfers between devices with their start and end apart: 3, of which 3 were waited for; matrix products, arithmetic and copies ran while one was open for 5% of the time, Pallas kernels for 0%

commit v1 on v0

v1 whole, which is shorter than its diff:
```python
import functools

import jax
import jax.numpy as jnp
from jax import lax
from jax.experimental import pallas as pl
from jax.experimental.pallas import tpu as pltpu
from jax.sharding import PartitionSpec as P

LANES = 256
CHUNKS = 8
UNROLL = 8


def split3(x):
    hi = x.astype(jnp.bfloat16)
    rest = x - hi.astype(jnp.float32)
    mid = rest.astype(jnp.bfloat16)
    lo = (rest - mid.astype(jnp.float32)).astype(jnp.bfloat16)
    return hi, mid, lo


def nt_dot(a, b):
    return lax.dot_general(a, b, (((1,), (1,)), ((), ())), preferred_element_type=jnp.float32)


def kernel(
    n,
    q_hbm,
    docs_hbm,
    lengths_hbm,
    cand_hbm,
    out_ref,
    docs,
    lengths,
    cand,
    queries,
    best,
    scores,
    table,
    doc_sem,
    small_sem,
    q_send,
    q_recv,
    s_send,
    s_recv,
):
    me = lax.axis_index("doc")
    count, doc_len, feature = docs.shape
    query_len = queries.shape[1]
    width = min(n, LANES // query_len)
    groups = n // width
    chunk = count // CHUNKS

    own = pltpu.make_async_copy(q_hbm.at[0], queries.at[me], small_sem.at[0])
    own.start()
    len_copy = pltpu.make_async_copy(lengths_hbm, lengths, small_sem.at[1])
    len_copy.start()
    doc_copies = []
    for c in range(CHUNKS):
        rows = pl.ds(c * chunk, chunk)
        copy = pltpu.make_async_copy(docs_hbm.at[rows], docs.at[rows], doc_sem.at[c])
        copy.start()
        doc_copies.append(copy)
    cand_copy = pltpu.make_async_copy(cand_hbm, cand, small_sem.at[2])
    cand_copy.start()

    barrier = pltpu.get_barrier_semaphore()

    @pl.loop(1, n)
    def _(p):
        pl.semaphore_signal(
            barrier,
            inc=1,
            device_id={"doc": lax.rem(me + p, n)},
            device_id_type=pl.DeviceIdType.MESH,
        )

    own.wait()
    pl.semaphore_wait(barrier, n - 1)

    def query_copy(peer, slot):
        return pltpu.make_async_remote_copy(
            src_ref=queries.at[me],
            dst_ref=queries.at[slot],
            send_sem=q_send.at[peer],
            recv_sem=q_recv.at[slot],
            device_id={"doc": peer},
            device_id_type=pl.DeviceIdType.MESH,
        )

    def score_copy(peer, slot):
        return pltpu.make_async_remote_copy(
            src_ref=scores.at[peer],
            dst_ref=table.at[slot],
            send_sem=s_send.at[peer],
            recv_sem=s_recv.at[slot],
            device_id={"doc": peer},
            device_id_type=pl.DeviceIdType.MESH,
        )

    home = me // width
    place = lax.rem(me, width)

    def peer_at(g, j):
        return lax.rem(home + g, groups) * width + lax.rem(place + j, width)

    @pl.loop(1, n)
    def _(p):
        query_copy(peer_at(p // width, lax.rem(p, width)), me).start()

    len_copy.wait()

    rows_of = lax.broadcasted_iota(jnp.int32, (doc_len, feature), 0)
    for c in range(CHUNKS):
        doc_copies[c].wait()

        @pl.loop(c * chunk, (c + 1) * chunk)
        def _(d):
            doc = docs[d]
            docs[d] = jnp.where(rows_of < lengths[0, d], doc, doc[0:1])

    lane_query = lax.broadcasted_iota(jnp.int32, (width, width * query_len), 1) // query_len
    row_query = lax.broadcasted_iota(jnp.int32, (width, width * query_len), 0)
    member = (lane_query == row_query).astype(jnp.bfloat16)

    @pl.loop(0, groups)
    def _(g):
        first = lax.rem(home + g, groups) * width

        @pl.loop(0, width)
        def _(j):
            @pl.when(first + j != me)
            def _():
                query_copy(first + j, first + j).wait_recv()

        q = queries[pl.ds(first, width)].reshape(width * query_len, feature)

        @pl.loop(0, count // UNROLL)
        def _(b):
            start = pl.multiple_of(b * UNROLL, UNROLL)
            parts = []
            for u in range(UNROLL):
                similar = nt_dot(docs[start + u], q)
                parts.append(jnp.max(similar, axis=0, keepdims=True))
            best[pl.ds(start, UNROLL), :] = jnp.concatenate(parts, axis=0)

        hi, mid, lo = split3(best[...])
        total = nt_dot(member, hi) + nt_dot(member, mid) + nt_dot(member, lo)
        for j in range(width):
            scores[first + j] = total[j : j + 1]

        @pl.loop(0, width)
        def _(j):
            peer = first + lax.rem(place + j, width)

            @pl.when(peer != me)
            def _():
                score_copy(peer, me).start()

    table[me] = scores[me]
    cand_copy.wait()

    @pl.loop(1, n)
    def _(p):
        peer = lax.rem(me + p, n)
        score_copy(peer, peer).wait_recv()

    ids = cand[...]
    owner = ids // count
    local = ids - owner * count
    cands = ids.shape[1]
    pick = (lax.broadcasted_iota(jnp.int32, (count, cands), 0) == local).astype(jnp.bfloat16)
    hi, mid, lo = split3(table[...].reshape(n, count))
    found = (
        jnp.dot(hi, pick, preferred_element_type=jnp.float32)
        + jnp.dot(mid, pick, preferred_element_type=jnp.float32)
        + jnp.dot(lo, pick, preferred_element_type=jnp.float32)
    )
    mine = lax.broadcasted_iota(jnp.int32, (n, cands), 0) == owner
    out_ref[...] = jnp.sum(jnp.where(mine, found, 0.0), axis=0, keepdims=True)

    @pl.loop(1, n)
    def _(p):
        peer = lax.rem(me + p, n)
        query_copy(peer, me).wait_send()
        score_copy(peer, me).wait_send()


def body(queries, doc_tokens, doc_lengths, candidates):
    n = lax.axis_size("doc")
    _, query_len, feature = queries.shape
    count, doc_len, _ = doc_tokens.shape
    cands = candidates.shape[1]
    width = min(n, LANES // query_len)
    hbm = pl.BlockSpec(memory_space=pl.ANY)
    return pl.pallas_call(
        functools.partial(kernel, n),
        out_shape=jax.ShapeDtypeStruct((1, cands), jnp.float32),
        in_specs=[hbm] * 4,
        out_specs=pl.BlockSpec(memory_space=pltpu.VMEM),
        scratch_shapes=[
            pltpu.VMEM((count, doc_len, feature), jnp.bfloat16),
            pltpu.SMEM((1, count), jnp.int32),
            pltpu.VMEM((1, cands), jnp.int32),
            pltpu.VMEM((n, query_len, feature), jnp.bfloat16),
            pltpu.VMEM((count, width * query_len), jnp.float32),
            pltpu.VMEM((n, 1, count), jnp.float32),
            pltpu.VMEM((n, 1, count), jnp.float32),
            pltpu.SemaphoreType.DMA((CHUNKS,)),
            pltpu.SemaphoreType.DMA((3,)),
            pltpu.SemaphoreType.DMA((n,)),
            pltpu.SemaphoreType.DMA((n,)),
            pltpu.SemaphoreType.DMA((n,)),
            pltpu.SemaphoreType.DMA((n,)),
        ],
        compiler_params=pltpu.CompilerParams(
            collective_id=0, has_side_effects=True, vmem_limit_bytes=32 * 1024 * 1024
        ),
        cost_estimate=pl.CostEstimate(
            flops=2 * n * query_len * count * doc_len * feature,
            bytes_accessed=2 * count * doc_len * feature,
            transcendentals=0,
        ),
        name="maxsim",
    )(queries, doc_tokens, doc_lengths.reshape(1, count), candidates)


def solution(mesh):
    placed = (
        P(("groups", "doc"), None, None),
        P(("groups", "doc"), None, None),
        P(("groups", "doc")),
        P(("groups", "doc"), None),
    )
    return jax.shard_map(
        body, mesh=mesh, in_specs=placed, out_specs=P(("groups", "doc"), None), check_vma=False
    )
```

time: 114 us -> 29.1 us (0.26)
  local copies, waits for them, and re-layouts: 54.9 us -> 4.78 us
  Pallas kernels: 0 us -> 24.1 us
  matrix products: 20.5 us -> 0 us
  waiting for transfers between devices: 15.1 us -> 0 us
  starting transfers between devices: 14.2 us -> 0 us
  other arithmetic: 8.09 us -> 0 us
    gather x13 -> x0, local copies, waits for them, and re-layouts: 49.1 us -> none  [the longest x4 40.7 us: score_block(): doc_block = doc_tokens[safe_docs]]
    pallas_call x0 -> x1, Pallas kernels: none -> 24.1 us  [body(): pl.pallas_call(functools.partial(kernel, n), out_shape=jax.ShapeDtypeStru...]
    dot_general x4 -> x0, matrix products: 20.5 us -> none  [score_block(): jnp.einsum('bak,bctk->bcat', block_queries.reshape(maxsim_width, query_le...]
    all_to_all x3 -> x0, waiting for transfers between devices: 15.1 us -> none  [the longest x1 6.36 us: body(): lax.all_to_all(got_scores, 'doc', split_axis=0, concat_axis=0, tiled=True)]
    all_to_all x3 -> x0, starting transfers between devices: 14.2 us -> none  [the longest x1 7.36 us: body(): lax.all_to_all(send_rows, 'doc', split_axis=0, concat_axis=0, tiled=True)]
    unnamed x2 -> x9, local copies, waits for them, and re-layouts: 0.84 us -> 4.78 us
    dynamic_update_slice x4 -> x0, other arithmetic: 2.41 us -> none  [body(): lax.map(score_block, (row_block.reshape(total_rows // maxsim_width, maxsi...]
    broadcast_in_dim x2 -> x0, local copies, waits for them, and re-layouts: 1.41 us -> none  [body(): jnp.broadcast_to(query_rows[None, :, :], (devices, local_queries, query_l...]
  transfers between devices with their start and end apart: 3 -> 0, of which waited for: 3 -> 0; matrix products, arithmetic and copies ran while one was open for 5% -> 0% of each run, Pallas kernels for 0% -> 0%
where the time goes in v1:
time: 29.1 us; the launch traced here: 28.9 us
  Pallas kernels  24.1 us (83%)
  local copies, waits for them, and re-layouts  4.78 us (16%)
    pallas_call x1, Pallas kernels, body(): pl.pallas_call(functools.partial(kernel, n), out_shape=jax.ShapeDtypeStru...  24.1 us
    unnamed x9, local copies, waits for them, and re-layouts  4.78 us

profile of v1, /device:TPU:0, one launch (start us, length us, event | category | flops | bytes accessed | tf_op | source)
XLA Modules:
  0.0 28.9 jit_solution(10518588399119585052)
XLA Ops:
  0.0 0.0 copy-start
  0.0 2.2 %copy-done = bf16[128,128,128]{2,1,0:T(8,128)(2,1)S(1)} copy-done((bf16[128,128,128]{2,1,0:T(8,128)(2,1)S(1)}, bf16[128,128,128]{2,1,0:T(8,128)(2,1)}, u32[]{:S(2)}) %copy-start) | copy-done | bytes 4194328
  2.2 0.0 copy-start.1
  2.2 0.7 %copy-done.1 = bf16[1,32,128]{2,1,0:T(8,128)(2,1)S(1)} copy-done((bf16[1,32,128]{2,1,0:T(8,128)(2,1)S(1)}, bf16[1,32,128]{2,1,0:T(8,128)(2,1)}, u32[]{:S(2)}) %copy-start.1) | copy-done | bytes 8216
  2.9 0.0 copy-start.2
  2.9 0.7 %copy-done.2 = s32[1,256]{1,0:T(1,128)S(1)} copy-done((s32[1,256]{1,0:T(1,128)S(1)}, s32[1,256]{1,0:T(1,128)}, u32[]{:S(2)}) %copy-start.2) | copy-done | bytes 1048
  3.6 0.0 copy-start.3
  3.6 0.7 %copy-done.3 = s32[128]{0:T(128)S(1)} copy-done((s32[128]{0:T(128)S(1)}, s32[128]{0:T(128)}, u32[]{:S(2)}) %copy-start.3) | copy-done | bytes 536
  4.2 24.1 %maxsim.1 = f32[1,256]{1,0:T(1,128)S(1)} custom-call(bf16[1,32,128]{2,1,0:T(8,128)(2,1)S(1)} %copy-done.1, bf16[128,128,128]{2,1,0:T(8,128)(2,1)S(1)} %copy-done, s32[1,128]{1,0:T(1,128)S(1)} %bitcast.1, s32[1,256]{1,0:T(1,128)S(1)} %copy-done.2), custom_call_target="tpu_custom_call" | custom-call | flops 2147483648 | bytes 4194304 | tf_op jit(solution)/shard_map/maxsim/pallas_call | solution.py:197
  28.3 0.6 %copy.6 = f32[1,256]{1,0:T(1,128)} copy(f32[1,256]{1,0:T(1,128)S(1)} %maxsim.1) | data formatting | bytes 2048
Async XLA Ops:
  0.0 2.2 %copy-start = (bf16[128,128,128]{2,1,0:T(8,128)(2,1)S(1)}, bf16[128,128,128]{2,1,0:T(8,128)(2,1)}, u32[]{:S(2)}) copy-start(bf16[128,128,128]{2,1,0:T(8,128)(2,1)} %docs_hbm.1) | copy-start | bytes 12582916
  2.2 0.7 %copy-start.1 = (bf16[1,32,128]{2,1,0:T(8,128)(2,1)S(1)}, bf16[1,32,128]{2,1,0:T(8,128)(2,1)}, u32[]{:S(2)}) copy-start(bf16[1,32,128]{2,1,0:T(8,128)(2,1)} %q_hbm.1) | copy-start | bytes 24580
  2.9 0.7 %copy-start.2 = (s32[1,256]{1,0:T(1,128)S(1)}, s32[1,256]{1,0:T(1,128)}, u32[]{:S(2)}) copy-start(s32[1,256]{1,0:T(1,128)} %cand_hbm.1) | copy-start | bytes 3076
  3.6 0.7 %copy-start.3 = (s32[128]{0:T(128)S(1)}, s32[128]{0:T(128)}, u32[]{:S(2)}) copy-start(s32[128]{0:T(128)} %param.6) | copy-start | bytes 1540

commit v2 on v1

--- a/solution.py
+++ b/solution.py
@@ -9,7 +9,7 @@
 
 LANES = 256
 CHUNKS = 8
-UNROLL = 8
+UNROLL = 64
 
 
 def split3(x):
@@ -50,18 +50,23 @@
     query_len = queries.shape[1]
     width = min(n, LANES // query_len)
     groups = n // width
+    home = me // width
+    place = lax.rem(me, width)
     chunk = count // CHUNKS
 
     own = pltpu.make_async_copy(q_hbm.at[0], queries.at[me], small_sem.at[0])
     own.start()
     len_copy = pltpu.make_async_copy(lengths_hbm, lengths, small_sem.at[1])
     len_copy.start()
-    doc_copies = []
-    for c in range(CHUNKS):
+
+    def doc_copy(c):
         rows = pl.ds(c * chunk, chunk)
-        copy = pltpu.make_async_copy(docs_hbm.at[rows], docs.at[rows], doc_sem.at[c])
-        copy.start()
-        doc_copies.append(copy)
+        return pltpu.make_async_copy(docs_hbm.at[rows], docs.at[rows], doc_sem.at[c])
+
+    @pl.loop(0, CHUNKS)
+    def _(c):
+        doc_copy(c).start()
+
     cand_copy = pltpu.make_async_copy(cand_hbm, cand, small_sem.at[2])
     cand_copy.start()
 
@@ -76,49 +81,53 @@
             device_id_type=pl.DeviceIdType.MESH,
         )
 
+    len_copy.wait()
+    rows_of = lax.broadcasted_iota(jnp.int32, (doc_len, feature), 0)
+
+    @pl.loop(0, CHUNKS)
+    def _(c):
+        doc_copy(c).wait()
+
+        @pl.loop(0, chunk, unroll=4)
+        def _(i):
+            d = c * chunk + i
+            doc = docs[d]
+            docs[d] = jnp.where(rows_of < lengths[0, d], doc, doc[0:1])
+
     own.wait()
     pl.semaphore_wait(barrier, n - 1)
 
-    def query_copy(peer, slot):
+    def query_copy(peer):
         return pltpu.make_async_remote_copy(
             src_ref=queries.at[me],
-            dst_ref=queries.at[slot],
-            send_sem=q_send.at[peer],
-            recv_sem=q_recv.at[slot],
+            dst_ref=queries.at[me],
+            send_sem=q_send.at[0],
+            recv_sem=q_recv.at[home],
             device_id={"doc": peer},
             device_id_type=pl.DeviceIdType.MESH,
         )
 
-    def score_copy(peer, slot):
+    def score_copy(peer):
         return pltpu.make_async_remote_copy(
             src_ref=scores.at[peer],
-            dst_ref=table.at[slot],
-            send_sem=s_send.at[peer],
-            recv_sem=s_recv.at[slot],
+            dst_ref=table.at[me],
+            send_sem=s_send.at[0],
+            recv_sem=s_recv.at[0],
             device_id={"doc": peer},
             device_id_type=pl.DeviceIdType.MESH,
         )
 
-    home = me // width
-    place = lax.rem(me, width)
+    def wait_slots(ref, slots, sem):
+        part = ref.at[pl.ds(0, slots)]
+        pltpu.make_async_copy(part, part, sem).wait()
+
 
     def peer_at(g, j):
         return lax.rem(home + g, groups) * width + lax.rem(place + j, width)
 
     @pl.loop(1, n)
     def _(p):
-        query_copy(peer_at(p // width, lax.rem(p, width)), me).start()
-
-    len_copy.wait()
-
-    rows_of = lax.broadcasted_iota(jnp.int32, (doc_len, feature), 0)
-    for c in range(CHUNKS):
-        doc_copies[c].wait()
-
-        @pl.loop(c * chunk, (c + 1) * chunk)
-        def _(d):
-            doc = docs[d]
-            docs[d] = jnp.where(rows_of < lengths[0, d], doc, doc[0:1])
+        query_copy(peer_at(p // width, lax.rem(p, width))).start()
 
     lane_query = lax.broadcasted_iota(jnp.int32, (width, width * query_len), 1) // query_len
     row_query = lax.broadcasted_iota(jnp.int32, (width, width * query_len), 0)
@@ -128,11 +137,13 @@
     def _(g):
         first = lax.rem(home + g, groups) * width
 
-        @pl.loop(0, width)
-        def _(j):
-            @pl.when(first + j != me)
-            def _():
-                query_copy(first + j, first + j).wait_recv()
+        @pl.when(g == 0)
+        def _():
+            wait_slots(queries, width - 1, q_recv.at[home])
+
+        @pl.when(g > 0)
+        def _():
+            wait_slots(queries, width, q_recv.at[first // width])
 
         q = queries[pl.ds(first, width)].reshape(width * query_len, feature)
 
@@ -156,15 +167,12 @@
 
             @pl.when(peer != me)
             def _():
-                score_copy(peer, me).start()
+                score_copy(peer).start()
 
     table[me] = scores[me]
     cand_copy.wait()
 
-    @pl.loop(1, n)
-    def _(p):
-        peer = lax.rem(me + p, n)
-        score_copy(peer, peer).wait_recv()
+    wait_slots(table, n - 1, s_recv.at[0])
 
     ids = cand[...]
     owner = ids // count
@@ -180,11 +188,8 @@
     mine = lax.broadcasted_iota(jnp.int32, (n, cands), 0) == owner
     out_ref[...] = jnp.sum(jnp.where(mine, found, 0.0), axis=0, keepdims=True)
 
-    @pl.loop(1, n)
-    def _(p):
-        peer = lax.rem(me + p, n)
-        query_copy(peer, me).wait_send()
-        score_copy(peer, me).wait_send()
+    wait_slots(queries, n - 1, q_send.at[0])
+    wait_slots(scores, n - 1, s_send.at[0])
 
 
 def body(queries, doc_tokens, doc_lengths, candidates):
@@ -209,13 +214,13 @@
             pltpu.VMEM((n, 1, count), jnp.float32),
             pltpu.SemaphoreType.DMA((CHUNKS,)),
             pltpu.SemaphoreType.DMA((3,)),
-            pltpu.SemaphoreType.DMA((n,)),
-            pltpu.SemaphoreType.DMA((n,)),
-            pltpu.SemaphoreType.DMA((n,)),
-            pltpu.SemaphoreType.DMA((n,)),
+            pltpu.SemaphoreType.DMA((1,)),
+            pltpu.SemaphoreType.DMA((n // width,)),
+            pltpu.SemaphoreType.DMA((1,)),
+            pltpu.SemaphoreType.DMA((1,)),
         ],
         compiler_params=pltpu.CompilerParams(
-            collective_id=0, has_side_effects=True, vmem_limit_bytes=32 * 1024 * 1024
+            collective_id=0, has_side_effects=True, vmem_limit_bytes=60 * 1024 * 1024
         ),
         cost_estimate=pl.CostEstimate(
             flops=2 * n * query_len * count * doc_len * feature,

time: 29.1 us -> 20.4 us (0.70)
  Pallas kernels: 24.1 us -> 19 us
  local copies, waits for them, and re-layouts: 4.78 us -> 1.24 us
    pallas_call x1, Pallas kernels: 24.1 us -> 19 us  [body(): pl.pallas_call(functools.partial(kernel, n), out_shape=jax.ShapeDtypeStru...]
    unnamed x9 -> x1, local copies, waits for them, and re-layouts: 4.78 us -> 1.24 us
where the time goes in v2:
time: 20.4 us; the launch traced here: 20.2 us
  Pallas kernels  19 us (93%)
  local copies, waits for them, and re-layouts  1.24 us (6%)
    pallas_call x1, Pallas kernels, body(): pl.pallas_call(functools.partial(kernel, n), out_shape=jax.ShapeDtypeStru...  19 us
    unnamed x1, local copies, waits for them, and re-layouts  1.24 us

profile of v2, /device:TPU:0, one launch (start us, length us, event | category | flops | bytes accessed | tf_op | source)
XLA Modules:
  0.0 20.2 jit_solution(11464474283775072179)
XLA Ops:
  0.0 19.0 %maxsim.1 = f32[1,256]{1,0:T(1,128)} custom-call(bf16[1,32,128]{2,1,0:T(8,128)(2,1)} %q_hbm.1, bf16[128,128,128]{2,1,0:T(8,128)(2,1)} %docs_hbm.1, s32[1,128]{1,0:T(1,128)} %bitcast.1, s32[1,256]{1,0:T(1,128)} %cand_hbm.1), custom_call_target="tpu_custom_call" | custom-call | flops 2147483648 | bytes 4194304 | tf_op jit(solution)/shard_map/maxsim/pallas_call | solution.py:202
  19.0 1.2 %copy.6 = f32[1,256]{1,0:T(1,128)} copy(f32[1,256]{1,0:T(1,128)} %maxsim.1) | data formatting | bytes 2048

commit v3 on v2

--- a/solution.py
+++ b/solution.py
@@ -9,7 +9,7 @@
 
 LANES = 256
 CHUNKS = 8
-UNROLL = 64
+UNROLL = 128
 
 
 def split3(x):
@@ -54,22 +54,6 @@
     place = lax.rem(me, width)
     chunk = count // CHUNKS
 
-    own = pltpu.make_async_copy(q_hbm.at[0], queries.at[me], small_sem.at[0])
-    own.start()
-    len_copy = pltpu.make_async_copy(lengths_hbm, lengths, small_sem.at[1])
-    len_copy.start()
-
-    def doc_copy(c):
-        rows = pl.ds(c * chunk, chunk)
-        return pltpu.make_async_copy(docs_hbm.at[rows], docs.at[rows], doc_sem.at[c])
-
-    @pl.loop(0, CHUNKS)
-    def _(c):
-        doc_copy(c).start()
-
-    cand_copy = pltpu.make_async_copy(cand_hbm, cand, small_sem.at[2])
-    cand_copy.start()
-
     barrier = pltpu.get_barrier_semaphore()
 
     @pl.loop(1, n)
@@ -81,18 +65,21 @@
             device_id_type=pl.DeviceIdType.MESH,
         )
 
-    len_copy.wait()
-    rows_of = lax.broadcasted_iota(jnp.int32, (doc_len, feature), 0)
+    own = pltpu.make_async_copy(q_hbm.at[0], queries.at[me], small_sem.at[0])
+    own.start()
+    len_copy = pltpu.make_async_copy(lengths_hbm, lengths, small_sem.at[1])
+    len_copy.start()
+
+    def doc_copy(c):
+        rows = pl.ds(c * chunk, chunk)
+        return pltpu.make_async_copy(docs_hbm.at[rows], docs.at[rows], doc_sem.at[c])
 
     @pl.loop(0, CHUNKS)
     def _(c):
-        doc_copy(c).wait()
-
-        @pl.loop(0, chunk, unroll=4)
-        def _(i):
-            d = c * chunk + i
-            doc = docs[d]
-            docs[d] = jnp.where(rows_of < lengths[0, d], doc, doc[0:1])
+        doc_copy(c).start()
+
+    cand_copy = pltpu.make_async_copy(cand_hbm, cand, small_sem.at[2])
+    cand_copy.start()
 
     own.wait()
     pl.semaphore_wait(barrier, n - 1)
@@ -121,13 +108,25 @@
         part = ref.at[pl.ds(0, slots)]
         pltpu.make_async_copy(part, part, sem).wait()
 
-
     def peer_at(g, j):
         return lax.rem(home + g, groups) * width + lax.rem(place + j, width)
 
     @pl.loop(1, n)
     def _(p):
         query_copy(peer_at(p // width, lax.rem(p, width))).start()
+
+    len_copy.wait()
+    rows_of = lax.broadcasted_iota(jnp.int32, (doc_len, feature), 0)
+
+    @pl.loop(0, CHUNKS)
+    def _(c):
+        doc_copy(c).wait()
+
+        @pl.loop(0, chunk, unroll=4)
+        def _(i):
+            d = c * chunk + i
+            doc = docs[d]
+            docs[d] = jnp.where(rows_of < lengths[0, d], doc, doc[0:1])
 
     lane_query = lax.broadcasted_iota(jnp.int32, (width, width * query_len), 1) // query_len
     row_query = lax.broadcasted_iota(jnp.int32, (width, width * query_len), 0)
@@ -172,13 +171,13 @@
     table[me] = scores[me]
     cand_copy.wait()
 
-    wait_slots(table, n - 1, s_recv.at[0])
 
     ids = cand[...]
     owner = ids // count
     local = ids - owner * count
     cands = ids.shape[1]
     pick = (lax.broadcasted_iota(jnp.int32, (count, cands), 0) == local).astype(jnp.bfloat16)
+    wait_slots(table, n - 1, s_recv.at[0])
     hi, mid, lo = split3(table[...].reshape(n, count))
     found = (
         jnp.dot(hi, pick, preferred_element_type=jnp.float32)

time: 20.4 us -> 20.2 us (level)
  Pallas kernels: 19 us -> 18.7 us
    pallas_call x1, Pallas kernels: 19 us -> 18.7 us  [body(): pl.pallas_call(functools.partial(kernel, n), out_shape=jax.ShapeDtypeStru...]
where the time goes in v3:
time: 20.2 us; the launch traced here: 20 us
  Pallas kernels  18.7 us (93%)
  local copies, waits for them, and re-layouts  1.24 us (6%)
    pallas_call x1, Pallas kernels, body(): pl.pallas_call(functools.partial(kernel, n), out_shape=jax.ShapeDtypeStru...  18.7 us
    unnamed x1, local copies, waits for them, and re-layouts  1.24 us

profile of v3, /device:TPU:0, one launch (start us, length us, event | category | flops | bytes accessed | tf_op | source)
XLA Modules:
  0.0 20.0 jit_solution(8073176813418827729)
XLA Ops:
  0.0 18.7 %maxsim.1 = f32[1,256]{1,0:T(1,128)} custom-call(bf16[1,32,128]{2,1,0:T(8,128)(2,1)} %q_hbm.1, bf16[128,128,128]{2,1,0:T(8,128)(2,1)} %docs_hbm.1, s32[1,128]{1,0:T(1,128)} %bitcast.1, s32[1,256]{1,0:T(1,128)} %cand_hbm.1), custom_call_target="tpu_custom_call" | custom-call | flops 2147483648 | bytes 4194304 | tf_op jit(solution)/shard_map/maxsim/pallas_call | solution.py:201
  18.7 1.2 %copy.6 = f32[1,256]{1,0:T(1,128)} copy(f32[1,256]{1,0:T(1,128)} %maxsim.1) | data formatting | bytes 2048

commit v4 on v3

--- a/solution.py
+++ b/solution.py
@@ -131,6 +131,7 @@
     lane_query = lax.broadcasted_iota(jnp.int32, (width, width * query_len), 1) // query_len
     row_query = lax.broadcasted_iota(jnp.int32, (width, width * query_len), 0)
     member = (lane_query == row_query).astype(jnp.bfloat16)
+    members = jnp.concatenate([member] * 3, axis=1)
 
     @pl.loop(0, groups)
     def _(g):
@@ -155,8 +156,7 @@
                 parts.append(jnp.max(similar, axis=0, keepdims=True))
             best[pl.ds(start, UNROLL), :] = jnp.concatenate(parts, axis=0)
 
-        hi, mid, lo = split3(best[...])
-        total = nt_dot(member, hi) + nt_dot(member, mid) + nt_dot(member, lo)
+        total = nt_dot(members, jnp.concatenate(split3(best[...]), axis=1))
         for j in range(width):
             scores[first + j] = total[j : j + 1]
 
@@ -178,12 +178,9 @@
     cands = ids.shape[1]
     pick = (lax.broadcasted_iota(jnp.int32, (count, cands), 0) == local).astype(jnp.bfloat16)
     wait_slots(table, n - 1, s_recv.at[0])
-    hi, mid, lo = split3(table[...].reshape(n, count))
-    found = (
-        jnp.dot(hi, pick, preferred_element_type=jnp.float32)
-        + jnp.dot(mid, pick, preferred_element_type=jnp.float32)
-        + jnp.dot(lo, pick, preferred_element_type=jnp.float32)
-    )
+    terms = jnp.concatenate(split3(table[...].reshape(n, count)), axis=0)
+    found = jnp.dot(terms, pick, preferred_element_type=jnp.float32)
+    found = found[:n] + found[n : 2 * n] + found[2 * n :]
     mine = lax.broadcasted_iota(jnp.int32, (n, cands), 0) == owner
     out_ref[...] = jnp.sum(jnp.where(mine, found, 0.0), axis=0, keepdims=True)
 

time: 20.2 us -> 20.2 us (level)
  no operation moved by 1% of the time
where the time goes in v4:
time: 20.2 us; the launch traced here: 20 us
  Pallas kernels  18.7 us (93%)
  local copies, waits for them, and re-layouts  1.24 us (6%)
    pallas_call x1, Pallas kernels, body(): pl.pallas_call(functools.partial(kernel, n), out_shape=jax.ShapeDtypeStru...  18.7 us
    unnamed x1, local copies, waits for them, and re-layouts  1.24 us

profile of v4, /device:TPU:0, one launch (start us, length us, event | category | flops | bytes accessed | tf_op | source)
XLA Modules:
  0.0 20.0 jit_solution(9923376069985865414)
XLA Ops:
  0.0 18.7 %maxsim.1 = f32[1,256]{1,0:T(1,128)} custom-call(bf16[1,32,128]{2,1,0:T(8,128)(2,1)} %q_hbm.1, bf16[128,128,128]{2,1,0:T(8,128)(2,1)} %docs_hbm.1, s32[1,128]{1,0:T(1,128)} %bitcast.1, s32[1,256]{1,0:T(1,128)} %cand_hbm.1), custom_call_target="tpu_custom_call" | custom-call | flops 2147483648 | bytes 4194304 | tf_op jit(solution)/shard_map/maxsim/pallas_call | solution.py:198
  18.7 1.2 %copy.6 = f32[1,256]{1,0:T(1,128)} copy(f32[1,256]{1,0:T(1,128)} %maxsim.1) | data formatting | bytes 2048
